TPU v7x, 32 devices: a whole 2x2x4 slice. The times are simulated.
32 devices in a mesh: ctx: 16 (over z, x, core), fsdp: 2 (over y).
Axes of the slice: x: 2, y: 2, z: 4, core: 2. Of those that a mesh axis runs over, the one named last changes fastest.
Arguments:
- tokens: bfloat16 [2, 6144, 576], P('fsdp', 'ctx'), may hold values from -6 to 6
- cotangent: bfloat16 [2, 6144, 576], P('fsdp', 'ctx'), may hold values from -6 to 6
- block_place: int32 [32], replicated, may hold values from 0 to 31, as said below
- norm_attn: bfloat16 [576], P('fsdp'), may hold values from 0.5 to 1.5
- w_query: bfloat16 [576, 576], P('fsdp'), may hold values from -0.25 to 0.25
- w_key: bfloat16 [576, 192], P('fsdp'), may hold values from -0.25 to 0.25
- w_value: bfloat16 [576, 192], P('fsdp'), may hold values from -0.25 to 0.25
- w_out: bfloat16 [576, 576], P('fsdp'), may hold values from -6 to 6
- norm_ffn: bfloat16 [576], P('fsdp'), may hold values from 0.5 to 1.5
- w_gate: bfloat16 [576, 1536], P('fsdp'), may hold values from -0.25 to 0.25
- w_up: bfloat16 [576, 1536], P('fsdp'), may hold values from -0.25 to 0.25
- w_down: bfloat16 [1536, 576], P('fsdp'), may hold values from -0.15625 to 0.15625
Outputs:
- layer_out: bfloat16 [2, 6144, 576], P('fsdp', 'ctx')
- grad_tokens: float32 [2, 6144, 576], P('fsdp', 'ctx')
- grad_norm_attn: float32 [576], P('fsdp')
- grad_w_query: float32 [576, 576], P('fsdp')
- grad_w_key: float32 [576, 192], P('fsdp')
- grad_w_value: float32 [576, 192], P('fsdp')
- grad_w_out: float32 [576, 576], P('fsdp')
- grad_norm_ffn: float32 [576], P('fsdp')
- grad_w_gate: float32 [576, 1536], P('fsdp')
- grad_w_up: float32 [576, 1536], P('fsdp')
- grad_w_down: float32 [1536, 576], P('fsdp')
Inputs may be any that keep to these rules, and one draw needn't show every extreme that they name: `block_place`: a permutation of the 32 blocks in which stored blocks 2i and 2i + 1 have places that add up to 31.
All inputs are finite; a program needn't handle non-finite values.
Results may differ from a plain program's by a relative error of at most 0.025.
Values may be sent and summed in bfloat16 or wider, within the bound.
A program may use at most 128 MiB of HBM per device.

v0:
```python
import jax
import jax.numpy as jnp
from jax import lax
from jax.sharding import PartitionSpec as P

HEADS = 9
KV_HEADS = 3


eps_norm = 1e-05
rope_base = 100000.0


def rope_tables(positions, width):
    steps = jnp.arange(width // 2, dtype=jnp.float32)
    freq = rope_base ** (-2.0 * steps / width)
    angle = positions.astype(jnp.float32)[:, None] * freq[None, :]
    return (jnp.cos(angle), jnp.sin(angle))


def rotate(v, cosine, sine):
    width = v.shape[-1] // 2
    first, second = (v[..., :width], v[..., width:])
    cosine = cosine[:, None, :]
    sine = sine[:, None, :]
    return jnp.concatenate([first * cosine - second * sine, second * cosine + first * sine], -1)


def normalize(v, gain):
    return v * lax.rsqrt(jnp.mean(v * v, -1, keepdims=True) + eps_norm) * gain


def norm_back(v, gain, grad):
    factor = lax.rsqrt(jnp.mean(v * v, -1, keepdims=True) + eps_norm)
    grad_gain = jnp.sum(grad * v * factor, 0)
    scaled = grad * gain
    grad_in = factor * scaled - v * factor**3 * jnp.mean(scaled * v, -1, keepdims=True)
    return (grad_in, grad_gain)


def inner(left, right):
    return lax.dot_general(
        left, right, (((0,), (0,)), ((), ())), preferred_element_type=jnp.float32
    )


def times_t(left, right):
    return lax.dot_general(
        left, right, (((1,), (1,)), ((), ())), preferred_element_type=jnp.float32
    )


def merge_block(carry, query, qpos, kblock, vblock, kpos, scale):
    top, total, accum = carry
    score = jnp.einsum("tgqd,sgd->gqts", query, kblock, preferred_element_type=jnp.float32) * scale
    allowed = (kpos[None, :] <= qpos[:, None])[None, None]
    new_top = jnp.maximum(top, jnp.max(jnp.where(allowed, score, -1e30), -1))
    weight = jnp.where(allowed, jnp.exp(score - new_top[..., None]), 0.0)
    fade = jnp.exp(top - new_top)
    total = total * fade + jnp.sum(weight, -1)
    accum = accum * fade[..., None] + jnp.einsum(
        "gqts,sgd->gqtd", weight.astype(jnp.bfloat16), vblock, preferred_element_type=jnp.float32
    )
    return (new_top, total, accum)


def body(
    tokens,
    cotangent,
    block_place,
    norm_attn,
    w_query,
    w_key,
    w_value,
    w_out,
    norm_ffn,
    w_gate,
    w_up,
    w_down,
):
    ctx_count = lax.axis_size("ctx")
    here = lax.axis_index("ctx")
    tok = tokens.shape[1]
    half = tok // 2
    length = tok * ctx_count
    groups = HEADS // KV_HEADS
    head = w_query.shape[1] // HEADS
    kv_width = KV_HEADS * head
    scale = head ** (-0.5)
    x_rows = tokens[0].astype(jnp.float32)
    gain_one, wq, wk, wv, wo, gain_two, wg, wu, wd = (
        lax.all_gather(norm_attn, "fsdp", axis=0, tiled=True),
        lax.all_gather(w_query, "fsdp", axis=0, tiled=True),
        lax.all_gather(w_key, "fsdp", axis=0, tiled=True),
        lax.all_gather(w_value, "fsdp", axis=0, tiled=True),
        lax.all_gather(w_out, "fsdp", axis=0, tiled=True),
        lax.all_gather(norm_ffn, "fsdp", axis=0, tiled=True),
        lax.all_gather(w_gate, "fsdp", axis=0, tiled=True),
        lax.all_gather(w_up, "fsdp", axis=0, tiled=True),
        lax.all_gather(w_down, "fsdp", axis=0, tiled=True),
    )
    gain_one = gain_one.astype(jnp.float32)
    gain_two = gain_two.astype(jnp.float32)
    rows = jnp.arange(length, dtype=jnp.int32)
    all_pos = block_place[rows // half] * half + rows % half
    my_pos = lax.dynamic_slice_in_dim(all_pos, here * tok, tok)
    cosine, sine = rope_tables(my_pos, head)
    normed = normalize(x_rows, gain_one).astype(jnp.bfloat16)
    q_raw = jnp.dot(normed, wq, preferred_element_type=jnp.float32)
    k_raw = jnp.dot(normed, wk, preferred_element_type=jnp.float32)
    values = jnp.dot(normed, wv, preferred_element_type=jnp.float32).astype(jnp.bfloat16)
    query = (
        rotate(q_raw.reshape(tok, HEADS, head), cosine, sine)
        .astype(jnp.bfloat16)
        .reshape(tok, KV_HEADS, groups, head)
    )
    keys = (
        rotate(k_raw.reshape(tok, KV_HEADS, head), cosine, sine)
        .astype(jnp.bfloat16)
        .reshape(tok, kv_width)
    )
    start_state = (
        jnp.full((KV_HEADS, groups, tok), -1e30, jnp.float32),
        jnp.zeros((KV_HEADS, groups, tok), jnp.float32),
        jnp.zeros((KV_HEADS, groups, tok, head), jnp.float32),
    )
    carry = start_state
    kpiece = lax.all_gather(keys, "ctx", axis=0, tiled=True)
    vpiece = lax.all_gather(values, "ctx", axis=0, tiled=True)
    count = kpiece.shape[0] // tok
    kblocks = kpiece.reshape(count, tok, KV_HEADS, head)
    vblocks = vpiece.reshape(count, tok, KV_HEADS, head)
    firsts = tok * jnp.arange(count, dtype=jnp.int32)

    def step(state, item):
        kblock, vblock, first = item
        kpos = lax.dynamic_slice_in_dim(all_pos, first, tok)
        return (merge_block(state, query, my_pos, kblock, vblock, kpos, scale), None)

    carry, unused = lax.scan(step, carry, (kblocks, vblocks, firsts))
    top, total, accum = carry
    lse = top + jnp.log(total)
    attn = accum / total[..., None]
    mixed = jnp.transpose(attn, (2, 0, 1, 3)).reshape(tok, HEADS * head).astype(jnp.bfloat16)
    middle = x_rows + jnp.dot(mixed, wo, preferred_element_type=jnp.float32)
    normed_two = normalize(middle, gain_two).astype(jnp.bfloat16)
    gate = jnp.dot(normed_two, wg, preferred_element_type=jnp.float32)
    upper = jnp.dot(normed_two, wu, preferred_element_type=jnp.float32)
    sig = jax.nn.sigmoid(gate)
    hidden = (gate * sig * upper).astype(jnp.bfloat16)
    result = middle + jnp.dot(hidden, wd, preferred_element_type=jnp.float32)
    seed_grad = cotangent[0]
    d_hidden = times_t(seed_grad, wd)
    grad_wd = inner(hidden, seed_grad)
    d_gate = (d_hidden * upper * sig * (1.0 + gate * (1.0 - sig))).astype(jnp.bfloat16)
    d_up = (d_hidden * gate * sig).astype(jnp.bfloat16)
    grad_wg = inner(normed_two, d_gate)
    grad_wu = inner(normed_two, d_up)
    d_norm_two = times_t(d_gate, wg) + times_t(d_up, wu)
    d_middle, grad_gain_two = norm_back(middle, gain_two, d_norm_two)
    d_middle = d_middle + seed_grad.astype(jnp.float32)
    d_branch = d_middle.astype(jnp.bfloat16)
    grad_wo = inner(mixed, d_branch)
    d_mixed = times_t(d_branch, wo).astype(jnp.bfloat16).reshape(tok, KV_HEADS, groups, head)
    delta = jnp.sum(jnp.transpose(d_mixed, (1, 2, 0, 3)).astype(jnp.float32) * attn, -1)
    back_k, back_v = (
        lax.all_gather(keys, "ctx", axis=0, tiled=True),
        lax.all_gather(values, "ctx", axis=0, tiled=True),
    )
    per_block = min(ctx_count, (511 + tok) // tok)
    key_rows = tok * per_block
    nblocks = ctx_count // per_block

    def score_grads(kblock, vblock, first, count):
        kpos = lax.dynamic_slice_in_dim(all_pos, first, count)
        score = (
            jnp.einsum("tgqd,sgd->gqts", query, kblock, preferred_element_type=jnp.float32) * scale
        )
        allowed = (kpos[None, :] <= my_pos[:, None])[None, None]
        prob = jnp.where(allowed, jnp.exp(score - lse[..., None]), 0.0)
        d_prob = jnp.einsum("tgqd,sgd->gqts", d_mixed, vblock, preferred_element_type=jnp.float32)
        d_score = (prob * (d_prob - delta[..., None])).astype(jnp.bfloat16)
        return (prob, d_score)

    def key_grads(prob, d_score, count):
        d_key = (
            jnp.einsum("gqts,tgqd->sgd", d_score, query, preferred_element_type=jnp.float32) * scale
        )
        d_value = jnp.einsum(
            "gqts,tgqd->sgd", prob.astype(jnp.bfloat16), d_mixed, preferred_element_type=jnp.float32
        )
        return (d_key.reshape(count, kv_width), d_value.reshape(count, kv_width))

    kblocks = back_k.reshape(nblocks, key_rows, KV_HEADS, head)
    vblocks = back_v.reshape(nblocks, key_rows, KV_HEADS, head)
    firsts = key_rows * jnp.arange(nblocks, dtype=jnp.int32)
    zero_query = jnp.zeros((tok, KV_HEADS, groups, head), jnp.float32)

    def back_step(d_query, item):
        kblock, vblock, first = item
        prob, d_score = score_grads(kblock, vblock, first, key_rows)
        d_query = (
            d_query
            + jnp.einsum("gqts,sgd->tgqd", d_score, kblock, preferred_element_type=jnp.float32)
            * scale
        )
        return (d_query, key_grads(prob, d_score, key_rows))

    d_query, key_terms = lax.scan(back_step, zero_query, (kblocks, vblocks, firsts))
    d_key_all = key_terms[0].reshape(length, kv_width)
    d_value_all = key_terms[1].reshape(length, kv_width)
    d_key_mine, d_value_mine = (
        lax.psum_scatter(
            d_key_all.astype(jnp.bfloat16), "ctx", scatter_dimension=0, tiled=True
        ).astype(jnp.float32),
        lax.psum_scatter(
            d_value_all.astype(jnp.bfloat16), "ctx", scatter_dimension=0, tiled=True
        ).astype(jnp.float32),
    )
    dq = (
        rotate(d_query.reshape(tok, HEADS, head), cosine, -sine)
        .astype(jnp.bfloat16)
        .reshape(tok, HEADS * head)
    )
    dk = (
        rotate(d_key_mine.reshape(tok, KV_HEADS, head), cosine, -sine)
        .astype(jnp.bfloat16)
        .reshape(tok, kv_width)
    )
    dv = d_value_mine.astype(jnp.bfloat16)
    grad_wq = inner(normed, dq)
    grad_wk = inner(normed, dk)
    grad_wv = inner(normed, dv)
    d_norm_one = times_t(dq, wq) + times_t(dk, wk) + times_t(dv, wv)
    d_input, grad_gain_one = norm_back(x_rows, gain_one, d_norm_one)
    grad_input = d_input + d_middle
    partials = (
        grad_gain_one,
        grad_wq,
        grad_wk,
        grad_wv,
        grad_wo,
        grad_gain_two,
        grad_wg,
        grad_wu,
        grad_wd,
    )
    summed = (
        lax.psum(partials[0].astype(jnp.bfloat16), "ctx").astype(jnp.float32),
        lax.psum(partials[1].astype(jnp.bfloat16), "ctx").astype(jnp.float32),
        lax.psum(partials[2].astype(jnp.bfloat16), "ctx").astype(jnp.float32),
        lax.psum(partials[3].astype(jnp.bfloat16), "ctx").astype(jnp.float32),
        lax.psum(partials[4].astype(jnp.bfloat16), "ctx").astype(jnp.float32),
        lax.psum(partials[5].astype(jnp.bfloat16), "ctx").astype(jnp.float32),
        lax.psum(partials[6].astype(jnp.bfloat16), "ctx").astype(jnp.float32),
        lax.psum(partials[7].astype(jnp.bfloat16), "ctx").astype(jnp.float32),
        lax.psum(partials[8].astype(jnp.bfloat16), "ctx").astype(jnp.float32),
    )
    owned = (
        lax.psum_scatter(
            summed[0].astype(jnp.bfloat16), "fsdp", scatter_dimension=0, tiled=True
        ).astype(jnp.float32),
        lax.psum_scatter(
            summed[1].astype(jnp.bfloat16), "fsdp", scatter_dimension=0, tiled=True
        ).astype(jnp.float32),
        lax.psum_scatter(
            summed[2].astype(jnp.bfloat16), "fsdp", scatter_dimension=0, tiled=True
        ).astype(jnp.float32),
        lax.psum_scatter(
            summed[3].astype(jnp.bfloat16), "fsdp", scatter_dimension=0, tiled=True
        ).astype(jnp.float32),
        lax.psum_scatter(
            summed[4].astype(jnp.bfloat16), "fsdp", scatter_dimension=0, tiled=True
        ).astype(jnp.float32),
        lax.psum_scatter(
            summed[5].astype(jnp.bfloat16), "fsdp", scatter_dimension=0, tiled=True
        ).astype(jnp.float32),
        lax.psum_scatter(
            summed[6].astype(jnp.bfloat16), "fsdp", scatter_dimension=0, tiled=True
        ).astype(jnp.float32),
        lax.psum_scatter(
            summed[7].astype(jnp.bfloat16), "fsdp", scatter_dimension=0, tiled=True
        ).astype(jnp.float32),
        lax.psum_scatter(
            summed[8].astype(jnp.bfloat16), "fsdp", scatter_dimension=0, tiled=True
        ).astype(jnp.float32),
    )
    return (
        result.astype(jnp.bfloat16)[None],
        grad_input[None],
        owned[0],
        owned[1],
        owned[2],
        owned[3],
        owned[4],
        owned[5],
        owned[6],
        owned[7],
        owned[8],
    )


def solution(mesh):
    placed = (
        P("fsdp", "ctx", None),
        P("fsdp", "ctx", None),
        P(),
        P("fsdp"),
        P("fsdp", None),
        P("fsdp", None),
        P("fsdp", None),
        P("fsdp", None),
        P("fsdp"),
        P("fsdp", None),
        P("fsdp", None),
        P("fsdp", None),
    )
    return jax.shard_map(
        body,
        mesh=mesh,
        in_specs=placed,
        out_specs=(
            P("fsdp", "ctx", None),
            P("fsdp", "ctx", None),
            P("fsdp"),
            P("fsdp", None),
            P("fsdp", None),
            P("fsdp", None),
            P("fsdp", None),
            P("fsdp"),
            P("fsdp", None),
            P("fsdp", None),
            P("fsdp", None),
        ),
        check_vma=False,
    )
```

profile of v0, /device:TPU:0, one launch (start us, length us, event | category | flops | bytes accessed | tf_op | source)
XLA Modules:
  0.0 882.7 jit_solution(16964218586340041208)
XLA Ops:
  12.2 5.8 all-reduce.7
  18.7 6.1 all_gather.39
  27.1 5.8 all_gather.36
  38.7 4.5 compare_select_fusion.1
  43.2 16.4 %fusion.79 = s32[6144]{0:T(1024)} fusion(pred[6144]{0:T(1024)(128)(4,1)S(1)} %compare_reduce_fusion, pred[6144]{0:T(1024)(128)(4,1)S(1)} %compare_reduce_fusion.1, pred[6144]{0:T(1024)(128)(4,1)S(1)} %compare_reduce_fusion.2, pred[6144]{0:T(1024)(128)(4,1)S(1)} %compare_reduce_fusion.3, pred[6144]{0:T(1024)(128)(4,1)S(1)} %compare_reduce_fusion.4, ...), kind=kLoop, calls=%fused_computation.164 | loop fusion | flops 202752 | bytes 202852 | tf_op jit(solution)/shard_map/add | solution.py:105
  64.9 8.4 all_gather.38
  73.3 8.9 %all_gather.41 = bf16[576,576]{1,0:T(8,128)(2,1)S(1)} all-gather(bf16[288,576]{1,0:T(8,128)(2,1)S(1)} %copy-done.39), channel_id=1, replica_groups=mesh['ctx'=16,'fsdp'=2] {'fsdp'}, dimensions={0}, use_global_device_ids=true | all-gather | bytes 995328 | tf_op jit(solution)/shard_map/all_gather | solution.py:96
  89.6 26.1 %all-gather.6.cloned.1.call-done = bf16[6144,192]{0,1:T(8,128)(2,1)} async-done(((bf16[384,192]{0,1:T(8,128)(2,1)}), bf16[6144,192]{0,1:T(8,128)(2,1)}) %all-gather.6.cloned.1.call-update) | async-done | bytes 2359312 | tf_op jit(solution)/shard_map/all_gather | solution.py:128
  119.8 155.9 %while.30 = (s32[]{:T(128)}, f32[3,3,384]{2,1,0:T(4,128)S(1)}, f32[3,3,384]{2,1,0:T(4,128)S(1)}, f32[3,3,384,64]{2,3,1,0:T(8,128)}, s32[16]{0:T(128)S(1)}, /*ind...) while((s32[]{:T(128)}, f32[3,3,384]{2,1,0:T(4,128)S(1)}, ...), condition=%wide.region_4.5_spmd.clone, body=%wide.region_1.4_spmd.clone.sunk | while | flops 355165056 | bytes 26327300 | solution.py:140
  291.7 6.1 multiply_convert_fusion
  307.1 142.4 %while.31 = (s32[]{:T(128)}, f32[384,3,3,64]{0,3,2,1:T(8,128)S(1)}, bf16[8,768,192]{1,2,0:T(8,128)(2,1)}, bf16[8,768,192]{1,2,0:T(8,128)(2,1)}, bf16[8,768,3,64]...) while((s32[]{:T(128)}, f32[384,3,3,64]{0,3,2,1:T(8,128)S(1)}, ...), condition=%wide.region_9.10_spmd.clone, body=%wide.region_8.9_spmd.clone.sunk | while | flops 1726488576 | bytes 56786236 | solution.py:209
  315.9 4.6 fusion.176
  333.6 4.6 fusion.176
  351.4 4.6 fusion.176
  369.1 4.6 fusion.176
  386.9 4.6 fusion.176
  404.7 4.6 fusion.176
  422.5 4.6 fusion.176
  440.3 4.6 fusion.176
  454.0 4.6 copy.70
  475.2 44.0 %reduce-scatter.28.cloned.1.call-done = bf16[384,192]{1,0:T(8,128)(2,1)} async-done(((bf16[6144,192]{1,0:T(8,128)(2,1)}), bf16[384,192]{1,0:T(8,128)(2,1)}) %reduce-scatter.28.cloned.1.call-update) | async-done | bytes 147472
  520.2 67.9 %reduce-scatter.30.cloned.1.call-done = bf16[384,192]{1,0:T(8,128)(2,1)} async-done(((bf16[6144,192]{1,0:T(8,128)(2,1)}), bf16[384,192]{1,0:T(8,128)(2,1)}) %reduce-scatter.30.cloned.1.call-update) | async-done | bytes 147472
  591.5 15.3 %reduce-scatter.20.cloned.1.call-done = bf16[288,576]{1,0:T(8,128)(2,1)} async-done(((bf16[576,576]{1,0:T(8,128)(2,1)}), bf16[288,576]{1,0:T(8,128)(2,1)}) %reduce-scatter.20.cloned.1.call-update) | async-done | bytes 331792 | tf_op jit(solution)/shard_map/reduce_scatter | solution.py:272
  606.8 19.8 %reduce-scatter.14.cloned.1.call-done = bf16[288,576]{1,0:T(8,128)(2,1)} async-done(((bf16[576,576]{1,0:T(8,128)(2,1)}), bf16[288,576]{1,0:T(8,128)(2,1)}) %reduce-scatter.14.cloned.1.call-update) | async-done | bytes 331792 | tf_op jit(solution)/shard_map/reduce_scatter | solution.py:263
  626.6 31.0 %reduce-scatter.26.cloned.1.call-done = bf16[768,576]{0,1:T(8,128)(2,1)} async-done(((bf16[1536,576]{0,1:T(8,128)(2,1)}), bf16[768,576]{0,1:T(8,128)(2,1)}) %reduce-scatter.26.cloned.1.call-update) | async-done | bytes 884752 | tf_op jit(solution)/shard_map/reduce_scatter | solution.py:284
  657.5 31.2 %reduce-scatter.24.cloned.1.call-done = bf16[288,1536]{1,0:T(8,128)(2,1)} async-done(((bf16[576,1536]{1,0:T(8,128)(2,1)}), bf16[288,1536]{1,0:T(8,128)(2,1)}) %reduce-scatter.24.cloned.1.call-update) | async-done | bytes 884752 | tf_op jit(solution)/shard_map/reduce_scatter | solution.py:281
  688.7 31.0 %reduce-scatter.22.cloned.1.call-done = bf16[288,1536]{1,0:T(8,128)(2,1)} async-done(((bf16[576,1536]{1,0:T(8,128)(2,1)}), bf16[288,1536]{1,0:T(8,128)(2,1)}) %reduce-scatter.22.cloned.1.call-update) | async-done | bytes 884752 | tf_op jit(solution)/shard_map/reduce_scatter | solution.py:278
  719.7 15.0 %reduce-scatter.18.cloned.1.call-done = bf16[288,192]{1,0:T(8,128)(2,1)} async-done(((bf16[576,192]{1,0:T(8,128)(2,1)}), bf16[288,192]{1,0:T(8,128)(2,1)}) %reduce-scatter.18.cloned.1.call-update) | async-done | bytes 110608 | tf_op jit(solution)/shard_map/reduce_scatter | solution.py:269
  734.6 14.8 %reduce-scatter.16.cloned.1.call-done = bf16[288,192]{1,0:T(8,128)(2,1)} async-done(((bf16[576,192]{1,0:T(8,128)(2,1)}), bf16[288,192]{1,0:T(8,128)(2,1)}) %reduce-scatter.16.cloned.1.call-update) | async-done | bytes 110608 | tf_op jit(solution)/shard_map/reduce_scatter | solution.py:266
  756.6 4.9 all-reduce.6
  761.7 32.8 %all-reduce.4 = (bf16[288]{0:T(512)(128)(2,1)S(1)}, bf16[288]{0:T(512)(128)(2,1)S(1)}) all-reduce(bf16[288]{0:T(512)(128)(2,1)S(1)} %dynamic-slice.3, bf16[288]{0:T(512)(128)(2,1)S(1)} %dynamic-slice.5), channel_id=1, replica_groups=mesh['ctx'=16,'fsdp'=2] {'ctx'}, use_global_device_ids=true, to_apply=%region_14.15 | all-reduce | flops 576 | bytes 2304 | tf_op jit(solution)/shard_map/psum | solution.py:249
  798.0 66.5 %all-reduce.10.cloned.1.call-done = (bf16[288,576]{1,0:T(8,128)(2,1)}, bf16[288,192]{1,0:T(8,128)(2,1)}, bf16[288,192]{1,0:T(8,128)(2,1)}, bf16[288,576]{1,0:T(8...) async-done(((bf16[288,576]{1,0:T(8,128)(2,1)}, bf16[288,192]{1,0:T(8,128)(2,1)}, bf16[288,192]{1,0:T(8,128)(2,1)}, ...) | async-done | bytes 3538960 | tf_op jit(solution)/shard_map/psum | solution.py:250
  (558 shorter events, 314.1 us)
Async XLA Ops:
  7.2 54.1 %copy-start = (bf16[1,384,576]{1,2,0:T(8,128)(2,1)S(1)}, bf16[1,384,576]{1,2,0:T(8,128)(2,1)}, u32[]{:S(2)}) copy-start(bf16[1,384,576]{1,2,0:T(8,128)(2,1)} %param.16) | copy-start | bytes 1327108
  7.2 19.9 %copy-start.41 = (bf16[288,192]{1,0:T(8,128)(2,1)S(1)}, bf16[288,192]{1,0:T(8,128)(2,1)}, u32[]{:S(2)}) copy-start(bf16[288,192]{1,0:T(8,128)(2,1)} %param.21) | copy-start | bytes 331780
  7.2 30.0 %copy-start.31 = (s32[32]{0:T(128)S(1)}, s32[32]{0:T(128)}, u32[]{:S(2)}) copy-start(s32[32]{0:T(128)} %param.18) | copy-start | bytes 388
  7.2 78.2 %all-gather.8.cloned.1.call-start = ((), (), s32[]{:S(2)}) async-start(), calls=%async_computation.10 | async-start | bytes 2506752 | tf_op jit(solution)/shard_map/all_gather | solution.py:129
  18.1 65.4 %copy-start.42 = (f32[576]{0:T(1024)}, f32[576]{0:T(1024)S(1)}, u32[]{:S(2)}) copy-start(f32[576]{0:T(1024)S(1)} %convert_element_type.208) | copy-start | bytes 6916
  18.7 64.8 %copy-start.44 = (f32[384]{0:T(512)}, f32[384]{0:T(512)S(1)}, u32[]{:S(2)}) copy-start(f32[384]{0:T(512)S(1)} %get-tuple-element.370) | copy-start | bytes 4612
  27.0 88.7 %all-gather.6.cloned.1.call-start = ((), (), s32[]{:S(2)}) async-start(), calls=%async_computation.9 | async-start | bytes 2506752 | tf_op jit(solution)/shard_map/all_gather | solution.py:128
  32.9 30.8 %copy-start.11 = (bf16[576,192]{1,0:T(8,128)(2,1)}, bf16[576,192]{1,0:T(8,128)(2,1)S(1)}, u32[]{:S(2)}) copy-start(bf16[576,192]{1,0:T(8,128)(2,1)S(1)} %all_gather.36) | copy-start | bytes 663556
  61.2 24.0 %copy-start.18 = (f32[384,32]{0,1:T(8,128)}, f32[384,32]{0,1:T(8,128)S(1)}, u32[]{:S(2)}) copy-start(f32[384,32]{0,1:T(8,128)S(1)} %get-tuple-element.368) | copy-start | bytes 147460
  61.6 11.7 %copy-start.39 = (bf16[288,576]{1,0:T(8,128)(2,1)S(1)}, bf16[288,576]{1,0:T(8,128)(2,1)}, u32[]{:S(2)}) copy-start(bf16[288,576]{1,0:T(8,128)(2,1)} %param.23) | copy-start | bytes 995332
  62.4 221.1 %all-gather.12.cloned.1.call-start = ((), (), s32[]{:S(2)}) async-start(), calls=%async_computation.12 | async-start | bytes 2654208 | tf_op jit(solution)/shard_map/all_gather | solution.py:99
  63.1 224.5 %all-gather.10.cloned.1.call-start = ((), (), s32[]{:S(2)}) async-start(), calls=%async_computation.11 | async-start | bytes 2654208 | tf_op jit(solution)/shard_map/all_gather | solution.py:98
  63.7 228.0 %all-gather.14.cloned.1.call-start = ((), (), s32[]{:S(2)}) async-start(), calls=%async_computation.13 | async-start | bytes 2654208 | tf_op jit(solution)/shard_map/all_gather | solution.py:100
  64.3 454.8 %reduce-scatter.28.cloned.1.call-start = ((), (), s32[]{:S(2)}) async-start(), calls=%async_computation.21 | async-start | bytes 3342336
  73.3 12.0 %copy-start.2 = (bf16[576,576]{1,0:T(8,128)(2,1)}, bf16[576,576]{1,0:T(8,128)(2,1)S(1)}, u32[]{:S(2)}) copy-start(bf16[576,576]{1,0:T(8,128)(2,1)S(1)} %all_gather.38) | copy-start | bytes 1990660
  82.2 199.2 %copy-start.4 = (bf16[576,576]{1,0:T(8,128)(2,1)}, bf16[576,576]{1,0:T(8,128)(2,1)S(1)}, u32[]{:S(2)}) copy-start(bf16[576,576]{1,0:T(8,128)(2,1)S(1)} %all_gather.41) | copy-start | bytes 1990660
  291.7 6.1 copy-start.50
  454.0 134.1 %reduce-scatter.30.cloned.1.call-start = ((), (), s32[]{:S(2)}) async-start(), calls=%async_computation.22 | async-start | bytes 3342336
  458.7 148.1 %reduce-scatter.20.cloned.1.call-start = ((), (), s32[]{:S(2)}) async-start(), calls=%async_computation.17 | async-start | bytes 1105920 | tf_op jit(solution)/shard_map/reduce_scatter | solution.py:272
  461.1 165.4 %reduce-scatter.14.cloned.1.call-start = ((), (), s32[]{:S(2)}) async-start(), calls=%async_computation.14 | async-start | bytes 1105920 | tf_op jit(solution)/shard_map/reduce_scatter | solution.py:263
  463.7 193.8 %reduce-scatter.26.cloned.1.call-start = ((), (), s32[]{:S(2)}) async-start(), calls=%async_computation.20 | async-start | bytes 2654208 | tf_op jit(solution)/shard_map/reduce_scatter | solution.py:284
  467.5 221.2 %reduce-scatter.24.cloned.1.call-start = ((), (), s32[]{:S(2)}) async-start(), calls=%async_computation.19 | async-start | bytes 2654208 | tf_op jit(solution)/shard_map/reduce_scatter | solution.py:281
  471.2 248.5 %reduce-scatter.22.cloned.1.call-start = ((), (), s32[]{:S(2)}) async-start(), calls=%async_computation.18 | async-start | bytes 2654208 | tf_op jit(solution)/shard_map/reduce_scatter | solution.py:278
  474.8 115.4 %copy-start.19 = (f32[384,32]{0,1:T(8,128)S(1)}, f32[384,32]{0,1:T(8,128)}, u32[]{:S(2)}) copy-start(f32[384,32]{0,1:T(8,128)} %copy-done.18) | copy-start | bytes 147460
  474.8 115.4 %copy-start.32 = (f32[384,32]{0,1:T(8,128)S(1)}, f32[384,32]{0,1:T(8,128)}, u32[]{:S(2)}) copy-start(f32[384,32]{0,1:T(8,128)} %get-tuple-element.366) | copy-start | bytes 147460
  474.8 259.8 %reduce-scatter.18.cloned.1.call-start = ((), (), s32[]{:S(2)}) async-start(), calls=%async_computation.16 | async-start | bytes 442368 | tf_op jit(solution)/shard_map/reduce_scatter | solution.py:269
  590.1 159.3 %reduce-scatter.16.cloned.1.call-start = ((), (), s32[]{:S(2)}) async-start(), calls=%async_computation.15 | async-start | bytes 442368 | tf_op jit(solution)/shard_map/reduce_scatter | solution.py:266
  590.3 159.2 %copy-start.29 = (bf16[384,3,64]{0,2,1:T(8,128)(2,1)}, bf16[384,3,64]{0,2,1:T(8,128)(2,1)S(1)}, u32[]{:S(2)}) copy-start(bf16[384,3,64]{0,2,1:T(8,128)(2,1)S(1)} %maximum_convert_fusion.1) | copy-start | bytes 442372
  591.4 273.1 %all-reduce.10.cloned.1.call-start = ((), (), s32[]{:S(2)}) async-start(), calls=%async_computation.23 | async-start | bytes 7372800 | tf_op jit(solution)/shard_map/psum | solution.py:250
  755.0 40.7 %copy-start.48 = (f32[384]{0:T(512)S(1)}, f32[384]{0:T(512)}, u32[]{:S(2)}) copy-start(f32[384]{0:T(512)} %get-tuple-element.369) | copy-start | bytes 4612
  864.5 7.2 copy-start.28
  867.8 5.3 copy-start.27
  (87 other events, 173.4 us)
Sparse Core Ops, SparseCore 0:
  27.1 44.3 all-gather.7
  74.3 41.3 all-gather.5
  117.2 28.1 all-gather.11
  146.8 29.4 all-gather.9
  177.7 29.4 all-gather.13
  454.1 65.0 reduce-scatter.27
  522.9 65.1 reduce-scatter.29
  590.9 15.8 reduce-scatter.19
  609.6 16.8 reduce-scatter.13
  629.2 28.2 reduce-scatter.25
  660.5 28.2 reduce-scatter.23
  691.4 28.2 reduce-scatter.21
  722.6 12.0 reduce-scatter.17
  737.4 12.0 reduce-scatter.15
  754.7 109.7 all-reduce.9
where the time goes:
time: 893 us; the launch traced here: 883 us
  waiting for transfers between devices  364 us (41%)
  matrix products  218 us (24%)
  local copies, waits for them, and re-layouts  90.1 us (10%)
  blocking collectives  72.8 us (8%)
  other arithmetic  71.9 us (8%)
  loops' own time  48.7 us (5%)
  between operations  16.1 us (2%)
    unnamed x17, waiting for transfers between devices  114 us
    psum x1, waiting for transfers between devices, body(): lax.psum(partials[1].astype(jnp.bfloat16), 'ctx').astype(jnp.float32)  66.5 us
    dot_general x8, matrix products, score_grads(): jnp.einsum('tgqd,sgd->gqts', d_mixed, vblock, preferred_element_type=jnp....  37 us
    dot_general x16, matrix products, merge_block(): jnp.einsum('gqts,sgd->gqtd', weight.astype(jnp.bfloat16), vblock, preferr...  35.9 us
    psum x1, blocking collectives, body(): lax.psum(partials[0].astype(jnp.bfloat16), 'ctx').astype(jnp.float32)  32.8 us
    unnamed x114, local copies, waits for them, and re-layouts  32.6 us
    another operation x1, loops' own time, body(): carry, unused = lax.scan(step, carry, (kblocks, vblocks, firsts))  32.2 us
    reduce_scatter x1, waiting for transfers between devices, body(): lax.psum_scatter(summed[7].astype(jnp.bfloat16), 'fsdp', scatter_dimensio...  31.2 us
  transfers between devices with their start and end apart: 15, of which 11 were waited for; matrix products, arithmetic and copies ran while one was open for 23% of the time, Pallas kernels for 0%

commit v1 on v0

v1 whole, which is shorter than its diff:
```python
import jax
import jax.numpy as jnp
from jax import lax
from jax.experimental import pallas as pl
from jax.experimental.pallas import tpu as pltpu
from jax.sharding import PartitionSpec as P

HEADS = 9
KV_HEADS = 3


eps_norm = 1e-05
rope_base = 100000.0


def rotate_t(v, cosine, sine):
    width = v.shape[-2] // 2
    first, second = (v[..., :width, :], v[..., width:, :])
    return jnp.concatenate([first * cosine - second * sine, second * cosine + first * sine], -2)


def normalize(v, gain):
    return v * lax.rsqrt(jnp.mean(v * v, -1, keepdims=True) + eps_norm) * gain


def norm_back(v, gain, grad):
    factor = lax.rsqrt(jnp.mean(v * v, -1, keepdims=True) + eps_norm)
    grad_gain = jnp.sum(grad * v * factor, 0)
    scaled = grad * gain
    grad_in = factor * scaled - v * factor**3 * jnp.mean(scaled * v, -1, keepdims=True)
    return (grad_in, grad_gain)


def inner(left, right):
    return lax.dot_general(
        left, right, (((0,), (0,)), ((), ())), preferred_element_type=jnp.float32
    )


def times_t(left, right):
    return lax.dot_general(
        left, right, (((1,), (1,)), ((), ())), preferred_element_type=jnp.float32
    )


def dot_tn(left, right):
    return lax.dot_general(
        left, right, (((0,), (0,)), ((), ())), preferred_element_type=jnp.float32
    )


def dot_nn(left, right):
    return jnp.dot(left, right, preferred_element_type=jnp.float32)


def causal(half, lanes, full):
    key = lax.broadcasted_iota(jnp.int32, (half, lanes), 0)
    lane = lax.broadcasted_iota(jnp.int32, (half, lanes), 1)
    return (key <= lax.rem(lane, half)) | (lane < full)


def over_blocks(place_ref, width, half, step):
    late, early = place_ref[0], place_ref[1]

    @pl.loop(0, early)
    def both(p):
        step(p, 2 * width, None)

    step(early, 2 * width, causal(half, 2 * width, width))

    @pl.loop(early + 1, late)
    def one(p):
        step(p, width, None)

    step(late, width, causal(half, width, 0))


def attend_kernel(stored_ref, place_ref, qt_ref, kv_ref, out_ref, lse_ref, top_ref, total_ref):
    kv_heads, head, lanes = out_ref.shape
    half = kv_ref.shape[2]
    top_ref[...] = jnp.full_like(top_ref, -1e30)
    total_ref[...] = jnp.zeros_like(total_ref)
    out_ref[...] = jnp.zeros_like(out_ref)

    def step(p, width, allowed):
        j = stored_ref[p]
        for g in range(kv_heads):
            kv = kv_ref[j, g]
            score = dot_nn(kv, qt_ref[g, :, :width])
            if allowed is not None:
                score = jnp.where(allowed, score, -1e30)
            top = top_ref[g, :, :width]
            new_top = jnp.maximum(top, jnp.max(score, 0, keepdims=True))
            weight = jnp.exp(score - new_top)
            fade = jnp.exp(top - new_top)
            top_ref[g, :, :width] = new_top
            total_ref[g, :, :width] = total_ref[g, :, :width] * fade + jnp.sum(
                weight, 0, keepdims=True
            )
            out_ref[g, :, :width] = (
                out_ref[g, :, :width] * fade + dot_tn(kv, weight.astype(jnp.bfloat16))[head:]
            )

    over_blocks(place_ref, lanes // 2, half, step)
    total = total_ref[...]
    lse_ref[...] = top_ref[...] + jnp.log(total)
    out_ref[...] = out_ref[...] / total


def attend_back_kernel(
    stored_ref, place_ref, qt_ref, qn_ref, dot_ref, don_ref, lse_ref, delta_ref, kv_ref,
    dq_ref, dkv_ref,
):
    kv_heads, head, lanes = dq_ref.shape
    half = kv_ref.shape[2]
    dq_ref[...] = jnp.zeros_like(dq_ref)

    def step(p, width, allowed):
        j = stored_ref[p]
        for g in range(kv_heads):
            kv = kv_ref[j, g]
            score = dot_nn(kv, qt_ref[g, :, :width])
            prob = jnp.exp(score - lse_ref[g, :, :width])
            if allowed is not None:
                prob = jnp.where(allowed, prob, 0.0)
            d_prob = dot_nn(kv, dot_ref[g, :, :width])
            d_score = (prob * (d_prob - delta_ref[g, :, :width])).astype(jnp.bfloat16)
            dkv_ref[j, g] = (
                dot_nn(d_score, qn_ref[g, :width]) + dot_nn(prob.astype(jnp.bfloat16), don_ref[g, :width])
            ).astype(jnp.bfloat16)
            dq_ref[g, :, :width] += dot_tn(kv, d_score)[:head]

    over_blocks(place_ref, lanes // 2, half, step)

    @pl.loop(place_ref[0] + 1, dkv_ref.shape[0])
    def unseen(p):
        dkv_ref[stored_ref[p]] = jnp.zeros(dkv_ref.shape[1:], dkv_ref.dtype)


def in_vmem(count):
    return [pl.BlockSpec(memory_space=pltpu.VMEM)] * count


def attend(stored, place, qt, kv):
    kv_heads, wide, lanes = qt.shape
    head = wide // 2
    work = kv.shape[0] * kv_heads * kv.shape[2] * lanes // 2
    return pl.pallas_call(
        attend_kernel,
        out_shape=(
            jax.ShapeDtypeStruct((kv_heads, head, lanes), jnp.float32),
            jax.ShapeDtypeStruct((kv_heads, 1, lanes), jnp.float32),
        ),
        in_specs=[pl.BlockSpec(memory_space=pltpu.SMEM)] * 2 + in_vmem(2),
        out_specs=tuple(in_vmem(2)),
        scratch_shapes=[pltpu.VMEM((kv_heads, 1, lanes), jnp.float32)] * 2,
        compiler_params=pltpu.CompilerParams(vmem_limit_bytes=48 << 20),
        cost_estimate=pl.CostEstimate(
            flops=4 * wide * work, bytes_accessed=2 * kv.size, transcendentals=work
        ),
        name="attend",
    )(stored, place, qt, kv)


def attend_back(stored, place, qt, qn, d_ot, d_on, lse, delta, kv):
    kv_heads, wide, lanes = qt.shape
    head = wide // 2
    work = kv.shape[0] * kv_heads * kv.shape[2] * lanes // 2
    return pl.pallas_call(
        attend_back_kernel,
        out_shape=(
            jax.ShapeDtypeStruct((kv_heads, head, lanes), jnp.float32),
            jax.ShapeDtypeStruct(kv.shape, jnp.bfloat16),
        ),
        in_specs=[pl.BlockSpec(memory_space=pltpu.SMEM)] * 2 + in_vmem(7),
        out_specs=tuple(in_vmem(2)),
        compiler_params=pltpu.CompilerParams(vmem_limit_bytes=48 << 20),
        cost_estimate=pl.CostEstimate(
            flops=10 * wide * work, bytes_accessed=4 * kv.size, transcendentals=work
        ),
        name="attend_back",
    )(stored, place, qt, qn, d_ot, d_on, lse, delta, kv)


def body(
    tokens,
    cotangent,
    block_place,
    norm_attn,
    w_query,
    w_key,
    w_value,
    w_out,
    norm_ffn,
    w_gate,
    w_up,
    w_down,
):
    here = lax.axis_index("ctx")
    tok = tokens.shape[1]
    half = tok // 2
    blocks = block_place.shape[0]
    groups = HEADS // KV_HEADS
    head = w_query.shape[1] // HEADS
    q_width = HEADS * head
    kv_width = KV_HEADS * head
    scale = head ** (-0.5)
    ff = w_gate.shape[1]

    mine = lax.dynamic_slice_in_dim(block_place, 2 * here, 2)
    swap = mine[0] < mine[1]
    place = jnp.where(swap, mine[::-1], mine)
    order = jnp.arange(blocks, dtype=jnp.int32)
    at = jnp.sum(jnp.where(block_place[None, :] == order[:, None], order[None, :], 0), 1)
    stored = (at // 2 * 2 + (order < blocks // 2)).astype(jnp.int32)

    def arrange(rows):
        return jnp.where(swap, jnp.concatenate([rows[half:], rows[:half]], 0), rows)

    first_pack = jnp.concatenate(
        [w_query, w_key, w_value, norm_attn[:, None], norm_ffn[:, None]], 1
    )
    first_pack = lax.all_gather(first_pack, "fsdp", axis=0, tiled=True)
    w_qkv = first_pack[:, : q_width + 2 * kv_width]
    gain_one = first_pack[:, -2].astype(jnp.float32)
    gain_two = first_pack[:, -1].astype(jnp.float32)

    x_rows = arrange(tokens[0]).astype(jnp.float32)
    seed_grad = arrange(cotangent[0])
    positions = (place[:, None] * half + jnp.arange(half, dtype=jnp.int32)[None, :]).reshape(tok)
    freq = rope_base ** (-2.0 * jnp.arange(head // 2, dtype=jnp.float32) / head)
    angle = freq[:, None] * positions.astype(jnp.float32)[None, :]
    cosine, sine = jnp.cos(angle), jnp.sin(angle)

    normed = normalize(x_rows, gain_one).astype(jnp.bfloat16)
    qkv_t = lax.dot_general(
        w_qkv, normed, (((0,), (1,)), ((), ())), preferred_element_type=jnp.float32
    )
    query = rotate_t(qkv_t[:q_width].reshape(HEADS, head, tok), cosine, sine).astype(jnp.bfloat16)
    keys = rotate_t(
        qkv_t[q_width : q_width + kv_width].reshape(KV_HEADS, head, tok), cosine, sine
    ).astype(jnp.bfloat16)
    values = qkv_t[q_width + kv_width :].reshape(KV_HEADS, head, tok).astype(jnp.bfloat16)
    kv = jnp.concatenate([keys, values], 1).reshape(KV_HEADS, 2 * head, 2, half)
    kv = lax.all_gather(jnp.transpose(kv, (2, 0, 3, 1)), "ctx", axis=0, tiled=True)

    def to_lanes(v):
        v = v.reshape(KV_HEADS, groups, head, 2, half)
        return jnp.transpose(v, (0, 2, 3, 1, 4)).reshape(KV_HEADS, head, 2 * groups * half)

    def from_lanes(v):
        v = v.reshape(KV_HEADS, head, 2, groups, half)
        return jnp.transpose(v, (0, 3, 1, 2, 4)).reshape(HEADS, head, tok)

    qt = to_lanes(query * jnp.bfloat16(scale))
    qt = jnp.concatenate([qt, jnp.zeros_like(qt)], 1)
    qn = jnp.swapaxes(qt, 1, 2)
    attn, lse = attend(stored, place, qt, kv)

    wo = lax.all_gather(w_out, "fsdp", axis=0, tiled=True)
    w_ff = lax.all_gather(jnp.concatenate([w_gate, w_up], 1), "fsdp", axis=0, tiled=True)
    wd = lax.all_gather(w_down, "fsdp", axis=0, tiled=True)

    mixed = jnp.transpose(from_lanes(attn.astype(jnp.bfloat16)).reshape(q_width, tok))
    middle = x_rows + dot_nn(mixed, wo)
    normed_two = normalize(middle, gain_two).astype(jnp.bfloat16)
    gate_up = dot_nn(normed_two, w_ff)
    gate, upper = gate_up[:, :ff], gate_up[:, ff:]
    sig = jax.nn.sigmoid(gate)
    hidden = (gate * sig * upper).astype(jnp.bfloat16)
    result = middle + dot_nn(hidden, wd)
    d_hidden = times_t(seed_grad, wd)
    grad_wd = inner(hidden, seed_grad).astype(jnp.bfloat16)
    d_gate = (d_hidden * upper * sig * (1.0 + gate * (1.0 - sig))).astype(jnp.bfloat16)
    d_up = (d_hidden * gate * sig).astype(jnp.bfloat16)
    d_ff = jnp.concatenate([d_gate, d_up], 1)
    grad_ff = inner(normed_two, d_ff).astype(jnp.bfloat16)
    d_norm_two = times_t(d_ff, w_ff)
    d_middle, grad_gain_two = norm_back(middle, gain_two, d_norm_two)
    d_middle = d_middle + seed_grad.astype(jnp.float32)
    d_branch = d_middle.astype(jnp.bfloat16)
    grad_wo = inner(mixed, d_branch).astype(jnp.bfloat16)
    d_mixed_t = times_t(wo, d_branch).astype(jnp.bfloat16)
    d_ot = to_lanes(d_mixed_t)
    delta = jnp.sum(d_ot.astype(jnp.float32) * attn, 1, keepdims=True)
    d_ot = jnp.concatenate([jnp.zeros_like(d_ot), d_ot], 1)
    d_on = jnp.swapaxes(d_ot, 1, 2)

    early = reduce_early(grad_wd, grad_ff, grad_wo)

    dqt, dkv = attend_back(stored, place, qt, qn, d_ot, d_on, lse, delta, kv)
    dkv = lax.psum_scatter(dkv, "ctx", scatter_dimension=0, tiled=True)
    dkv = jnp.transpose(dkv, (1, 3, 0, 2)).reshape(KV_HEADS, 2 * head, tok)
    dk_t = dkv[:, :head].astype(jnp.float32)
    dq_t = from_lanes(dqt) * scale
    d_qkv_t = jnp.concatenate(
        [
            rotate_t(dq_t, cosine, -sine).astype(jnp.bfloat16).reshape(q_width, tok),
            rotate_t(dk_t, cosine, -sine).astype(jnp.bfloat16).reshape(kv_width, tok),
            dkv[:, head:].reshape(kv_width, tok),
        ],
        0,
    )
    grad_qkv = jnp.transpose(dot_nn(d_qkv_t, normed)).astype(jnp.bfloat16)
    d_norm_one = lax.dot_general(
        d_qkv_t, w_qkv, (((0,), (1,)), ((), ())), preferred_element_type=jnp.float32
    )
    d_input, grad_gain_one = norm_back(x_rows, gain_one, d_norm_one)
    grad_input = d_input + d_middle
    late = reduce_late(grad_qkv, grad_gain_one, grad_gain_two)

    grad_wd, grad_ff, grad_wo = early
    grad_qkv, grad_gain_one, grad_gain_two = late
    return (
        arrange(result.astype(jnp.bfloat16))[None],
        arrange(grad_input)[None],
        grad_gain_one,
        grad_qkv[:, :q_width],
        grad_qkv[:, q_width : q_width + kv_width],
        grad_qkv[:, q_width + kv_width :],
        grad_wo,
        grad_gain_two,
        grad_ff[:, :ff],
        grad_ff[:, ff:],
        grad_wd,
    )


def reduce_early(grad_wd, grad_ff, grad_wo):
    def total(v):
        v = lax.psum_scatter(v, "fsdp", scatter_dimension=0, tiled=True)
        return lax.psum(v, "ctx").astype(jnp.float32)

    return total(grad_wd), total(grad_ff), total(grad_wo)


def reduce_late(grad_qkv, grad_gain_one, grad_gain_two):
    gains = jnp.stack([grad_gain_one, grad_gain_two], 1).astype(jnp.bfloat16)
    pack = jnp.concatenate([grad_qkv, gains], 1)
    pack = lax.psum_scatter(pack, "fsdp", scatter_dimension=0, tiled=True)
    pack = lax.psum(pack, "ctx").astype(jnp.float32)
    return pack[:, :-2], pack[:, -2], pack[:, -1]


def solution(mesh):
    placed = (
        P("fsdp", "ctx", None),
        P("fsdp", "ctx", None),
        P(),
        P("fsdp"),
        P("fsdp", None),
        P("fsdp", None),
        P("fsdp", None),
        P("fsdp", None),
        P("fsdp"),
        P("fsdp", None),
        P("fsdp", None),
        P("fsdp", None),
    )
    return jax.shard_map(
        body,
        mesh=mesh,
        in_specs=placed,
        out_specs=(
            P("fsdp", "ctx", None),
            P("fsdp", "ctx", None),
            P("fsdp"),
            P("fsdp", None),
            P("fsdp", None),
            P("fsdp", None),
            P("fsdp", None),
            P("fsdp"),
            P("fsdp", None),
            P("fsdp", None),
            P("fsdp", None),
        ),
        check_vma=False,
    )
```

time: 893 us -> 578 us (0.65)
  matrix products: 218 us -> 36.9 us
  Pallas kernels: 0 us -> 72 us
  blocking collectives: 72.8 us -> 11.1 us
  other arithmetic: 71.9 us -> 23 us
  loops' own time: 48.7 us -> 0 us
  local copies, waits for them, and re-layouts: 90.1 us -> 47.4 us
    dot_general x79 -> x6, matrix products: 190 us -> 16.7 us  [the longest x4 12.1 us: dot_nn(): return jnp.dot(left, right, preferred_element_type=jnp.float32)]
    unnamed x17 -> x10, waiting for transfers between devices: 114 us -> 0.67 us
    pallas_call x0 -> x2, Pallas kernels: none -> 72 us  [the longest x1 38.5 us: attend_back(): pl.pallas_call(attend_back_kernel, out_shape=(jax.ShapeDtypeStruct((kv_he...]
    all_gather x5 -> x4, waiting for transfers between devices: 26.1 us -> 86.9 us  [the longest x1 34.6 us: body(): lax.all_gather(jnp.transpose(kv, (2, 0, 3, 1)), 'ctx', axis=0, tiled=True)]
    another operation x2 -> x0, loops' own time: 48.7 us -> none  [the longest x1 32.2 us: body(): carry, unused = lax.scan(step, carry, (kblocks, vblocks, firsts))]
    psum x1, waiting for transfers between devices: 66.5 us -> 105 us  [reduce_late(): pack = lax.psum(pack, 'ctx').astype(jnp.float32)]
    psum x1 -> x0, blocking collectives: 32.8 us -> none  [body(): lax.psum(partials[0].astype(jnp.bfloat16), 'ctx').astype(jnp.float32)]
    dynamic_slice x48 -> x1, local copies, waits for them, and re-layouts: 32.6 us -> 0.08 us  [body(): mine = lax.dynamic_slice_in_dim(block_place, 2 * here, 2)]
  transfers between devices with their start and end apart: 15 -> 10, of which waited for: 11 -> 10; matrix products, arithmetic and copies ran while one was open for 23% -> 10% of each run, Pallas kernels for 0% -> 6%
where the time goes in v1:
time: 578 us; the launch traced here: 570 us
  waiting for transfers between devices  363 us (63%)
  Pallas kernels  72 us (12%)
  local copies, waits for them, and re-layouts  47.4 us (8%)
  matrix products  36.9 us (6%)
  other arithmetic  23 us (4%)
  between operations  16.6 us (3%)
  blocking collectives  11.1 us (2%)
    psum x1, waiting for transfers between devices, reduce_late(): pack = lax.psum(pack, 'ctx').astype(jnp.float32)  105 us
    reduce_scatter x3, waiting for transfers between devices, total(): v = lax.psum_scatter(v, 'fsdp', scatter_dimension=0, tiled=True)  92.2 us
    reduce_scatter x1, waiting for transfers between devices, body(): dkv = lax.psum_scatter(dkv, 'ctx', scatter_dimension=0, tiled=True)  52.8 us
    pallas_call x1, Pallas kernels, attend_back(): pl.pallas_call(attend_back_kernel, out_shape=(jax.ShapeDtypeStruct((kv_he...  38.5 us
    all_gather x1, waiting for transfers between devices, body(): lax.all_gather(jnp.transpose(kv, (2, 0, 3, 1)), 'ctx', axis=0, tiled=True)  34.6 us
    pallas_call x1, Pallas kernels, attend(): pl.pallas_call(attend_kernel, out_shape=(jax.ShapeDtypeStruct((kv_heads,...  33.5 us
    reduce_scatter x1, waiting for transfers between devices, reduce_late(): pack = lax.psum_scatter(pack, 'fsdp', scatter_dimension=0, tiled=True)  24.7 us
    all_gather x1, waiting for transfers between devices, body(): wd = lax.all_gather(w_down, 'fsdp', axis=0, tiled=True)  24.6 us
  transfers between devices with their start and end apart: 10, of which 10 were waited for; matrix products, arithmetic and copies ran while one was open for 10% of the time, Pallas kernels for 6%

profile of v1, /device:TPU:0, one launch (start us, length us, event | category | flops | bytes accessed | tf_op | source)
XLA Modules:
  0.0 570.2 jit_solution(1094791508157416806)
XLA Ops:
  8.9 2.0 concatenate.64
  16.2 20.3 %all-gather.5.cloned.1.call-done = bf16[576,962]{1,0:T(8,128)(2,1)} async-done(((bf16[288,962]{1,0:T(8,128)(2,1)}), bf16[576,962]{1,0:T(8,128)(2,1)}) %all-gather.5.cloned.1.call-update) | async-done | bytes 1108240 | tf_op jit(solution)/shard_map/all_gather | solution.py:223
  37.9 2.3 fusion.5
  45.9 2.6 pad_maximum_fusion.1
  49.5 11.1 %all_gather.17 = bf16[576,576]{1,0:T(8,128)(2,1)} all-gather(bf16[288,576]{1,0:T(8,128)(2,1)S(1)} %copy-done.30), channel_id=1, replica_groups=mesh['ctx'=16,'fsdp'=2] {'fsdp'}, dimensions={0}, use_global_device_ids=true | all-gather | bytes 995328 | tf_op jit(solution)/shard_map/all_gather | solution.py:260
  64.6 34.6 %all-gather.7.cloned.1.call-done.kv_ref = bf16[32,3,192,128]{3,2,1,0:T(8,128)(2,1)} async-done(((bf16[2,3,192,128]{3,2,1,0:T(8,128)(2,1)}), bf16[32,3,192,128]{3,2,1,0:T(8,128)(2,1)}) %all-gather.7.cloned.1.call-update) | async-done | bytes 4718608 | tf_op jit(solution)/shard_map/all_gather | solution.py:245
  99.2 33.5 %attend.1 = (f32[3,64,1152]{2,1,0:T(8,128)S(1)}, f32[3,1,1152]{2,1,0:T(1,128)S(1)}) custom-call(s32[32]{0:T(128)S(1)} %fusion.24.stored_ref, s32[2]{0:T(128)S(1)} %get-tuple-element.32.place_ref, bf16[3,128,1152]{2,1,0:T(8,128)(2,1)S(1)} %concatenate.68.clone.qt_ref, bf16[32,3,192,128]{3,2,1,0:T(8,128)(2,1)} %all-gather.7.cloned.1.call-done.kv_ref), custom_call_target="tpu_custom_call" | custom-call | flops 5435817984 | bytes 4718592 | tf_op jit(solution)/shard_map/attend/pallas_call | solution.py:148
  133.5 2.2 reshape.236
  137.1 2.2 reshape_reshape.3
  139.3 2.0 multiply_reduce_fusion.3
  141.9 7.3 %all-gather.9.cloned.1.call-done = bf16[576,3072]{1,0:T(8,128)(2,1)} async-done(((bf16[288,3072]{1,0:T(8,128)(2,1)}), bf16[576,3072]{1,0:T(8,128)(2,1)}) %all-gather.9.cloned.1.call-update) | async-done | bytes 3538960 | tf_op jit(solution)/shard_map/all_gather | solution.py:261
  149.3 6.3 %fusion.29 = f32[384,3072]{1,0:T(8,128)} fusion(bf16[576,3072]{1,0:T(8,128)(2,1)} %all-gather.9.cloned.1.call-done, f32[384,576]{0,1:T(8,128)S(1)} %get-tuple-element.72, f32[576]{0:T(1024)S(1)} %get-tuple-element.25, f32[384]{0:T(512)S(1)} %get-tuple-element.68), kind=kOutput, calls=%fused_computation.99 | convolution fusion | flops 1359618048 | bytes 9146112 | tf_op jit(solution)/shard_map/dot_general | solution.py:53
  155.5 24.6 %all-gather.11.cloned.1.call-done = bf16[1536,576]{0,1:T(8,128)(2,1)} async-done(((bf16[768,576]{0,1:T(8,128)(2,1)}), bf16[1536,576]{0,1:T(8,128)(2,1)}) %all-gather.11.cloned.1.call-update) | async-done | bytes 1769488 | tf_op jit(solution)/shard_map/all_gather | solution.py:262
  180.1 6.2 %multiply_convert_fusion.1 = (bf16[384,1536]{1,0:T(8,128)(2,1)S(1)}, bf16[384,1536]{1,0:T(8,128)(2,1)S(1)}, bf16[384,1536]{1,0:T(8,128)(2,1)}) fusion(f32[384,3072]{1,0:T(8,128)} %fusion.29, bf16[384,576]{0,1:T(8,128)(2,1)} %maximum_select_fusion.3, bf16[1536,576]{0,1:T(8,128)(2,1)} %all-gather.11.cloned.1.call-done), kind=kOutput, calls=%fused_computation.4 | convolution fusion | flops 688914432 | bytes 10469376 | tf_op jit(solution)/shard_map/dot_general | solution.py:41
  186.4 2.7 multiply_reduce_fusion.1
  192.1 2.3 copy.111
  201.0 2.0 multiply_reduce_fusion
  203.0 38.5 %attend_back.1 = (f32[3,64,1152]{2,1,0:T(8,128)S(1)}, bf16[32,3,192,128]{3,2,1,0:T(8,128)(2,1)}) custom-call(s32[32]{0:T(128)S(1)} %fusion.24.stored_ref, s32[2]{0:T(128)S(1)} %get-tuple-element.32.place_ref, bf16[3,128,1152]{2,1,0:T(8,128)(2,1)S(1)} %concatenate.68.clone.qt_ref, bf16[3,1152,128]{2,1,0:T(8,128)(2,1)S(1)} %pad_bitcast_fusion.1.qn_ref, ...), custom_call_target="tpu_custom_call" | custom-call | flops 13589544960 | bytes 9437184 | tf_op jit(solution)/shard_map/attend_back/pallas_call | solution.py:169
  244.3 3.6 convolution_convert_fusion.1
  249.1 5.6 convolution_convert_fusion
  256.3 2.2 mul.362
  258.6 3.2 copy.115
  261.7 2.3 mul.364
  265.8 52.8 %reduce-scatter.6.cloned.1.call-done = bf16[2,3,192,128]{3,2,1,0:T(8,128)(2,1)} async-done(((bf16[32,3,192,128]{3,2,1,0:T(8,128)(2,1)}), bf16[2,3,192,128]{3,2,1,0:T(8,128)(2,1)}) %reduce-scatter.6.cloned.1.call-update) | async-done | bytes 294928 | tf_op jit(solution)/shard_map/reduce_scatter | solution.py:292
  321.6 2.4 fusion.15
  326.4 11.0 %reduce-scatter.10.cloned.1.call-done = bf16[288,576]{1,0:T(8,128)(2,1)} async-done(((bf16[576,576]{1,0:T(8,128)(2,1)}), bf16[288,576]{1,0:T(8,128)(2,1)}) %reduce-scatter.10.cloned.1.call-update) | async-done | bytes 331792 | tf_op jit(solution)/shard_map/reduce_scatter | solution.py:331
  337.4 31.2 %reduce-scatter.14.cloned.1.call-done = bf16[768,576]{0,1:T(8,128)(2,1)} async-done(((bf16[1536,576]{0,1:T(8,128)(2,1)}), bf16[768,576]{0,1:T(8,128)(2,1)}) %reduce-scatter.14.cloned.1.call-update) | async-done | bytes 884752 | tf_op jit(solution)/shard_map/reduce_scatter | solution.py:331
  368.6 50.0 %reduce-scatter.12.cloned.1.call-done = bf16[288,3072]{1,0:T(8,128)(2,1)} async-done(((bf16[576,3072]{1,0:T(8,128)(2,1)}), bf16[288,3072]{1,0:T(8,128)(2,1)}) %reduce-scatter.12.cloned.1.call-update) | async-done | bytes 1769488 | tf_op jit(solution)/shard_map/reduce_scatter | solution.py:331
  418.5 24.7 %reduce-scatter.8.cloned.1.call-done = bf16[288,962]{1,0:T(8,128)(2,1)} async-done(((bf16[576,962]{1,0:T(8,128)(2,1)}), bf16[288,962]{1,0:T(8,128)(2,1)}) %reduce-scatter.8.cloned.1.call-update) | async-done | bytes 554128 | tf_op jit(solution)/shard_map/reduce_scatter | solution.py:340
  443.3 2.9 fusion.1
  449.0 105.4 %all-reduce.5.cloned.1.call-done = (bf16[288,962]{1,0:T(8,128)(2,1)}, bf16[288,576]{1,0:T(8,128)(2,1)}, bf16[288,3072]{1,0:T(8,128)(2,1)}, bf16[768,576]{0,1:T(8,128)(2,1)}) async-done(((bf16[288,962]{1,0:T(8,128)(2,1)}, bf16[288,576]{1,0:T(8,128)(2,1)}, bf16[288,3072]{1,0:T(8,128)(2,1)}, bf16[768,576]{0,1:T(8,128)(2,1)}), (bf16[288,962]{1,0:T(8,128)(2,1)}, bf16[288,576]{1,0:T(8,128)(2,1)}, ...) | async-done | bytes 3540112 | tf_op jit(solution)/shard_map/psum | solution.py:341
  559.3 2.3 fusion.30
  (185 shorter events, 51.3 us)
Async XLA Ops:
  7.2 3.8 copy-start.40
  7.2 7.9 %copy-start.15 = (bf16[1,384,576]{1,2,0:T(8,128)(2,1)S(1)}, bf16[1,384,576]{1,2,0:T(8,128)(2,1)}, u32[]{:S(2)}) copy-start(bf16[1,384,576]{1,2,0:T(8,128)(2,1)} %param.12) | copy-start | bytes 1327108
  7.2 29.4 %all-gather.5.cloned.1.call-start = ((), (), s32[]{:S(2)}) async-start(), calls=%async_computation.5 | async-start | bytes 1769472 | tf_op jit(solution)/shard_map/all_gather | solution.py:223
  10.9 88.2 %all-gather.7.cloned.1.call-start = ((), (), s32[]{:S(2)}) async-start(), calls=%async_computation.6 | async-start | bytes 5013504 | tf_op jit(solution)/shard_map/all_gather | solution.py:245
  14.2 47.6 %copy-start.23 = (f32[32,384]{1,0:T(8,128)}, f32[32,384]{1,0:T(8,128)S(1)}, u32[]{:S(2)}) copy-start(f32[32,384]{1,0:T(8,128)S(1)} %get-tuple-element.64) | copy-start | bytes 147460
  15.1 26.4 %copy-start.17 = (f32[32,384]{0,1:T(8,128)}, f32[32,384]{0,1:T(8,128)S(1)}, u32[]{:S(2)}) copy-start(f32[32,384]{0,1:T(8,128)S(1)} %copy.103) | copy-start | bytes 147460
  15.6 24.5 %copy-start.13 = (bf16[384,576]{0,1:T(8,128)(2,1)}, bf16[384,576]{0,1:T(8,128)(2,1)S(1)}, u32[]{:S(2)}) copy-start(bf16[384,576]{0,1:T(8,128)(2,1)S(1)} %get-tuple-element.34) | copy-start | bytes 1327108
  16.2 21.6 %copy-start.36 = (f32[384]{0:T(512)}, f32[384]{0:T(512)S(1)}, u32[]{:S(2)}) copy-start(f32[384]{0:T(512)S(1)} %get-tuple-element.66) | copy-start | bytes 4612
  42.6 3.2 copy-start.21
  45.8 103.5 %all-gather.9.cloned.1.call-start = ((), (), s32[]{:S(2)}) async-start(), calls=%async_computation.7 | async-start | bytes 5308416 | tf_op jit(solution)/shard_map/all_gather | solution.py:261
  48.5 12.1 %copy-start.16 = (bf16[1,384,576]{1,2,0:T(8,128)(2,1)S(1)}, bf16[1,384,576]{1,2,0:T(8,128)(2,1)}, u32[]{:S(2)}) copy-start(bf16[1,384,576]{1,2,0:T(8,128)(2,1)} %param.13) | copy-start | bytes 1327108
  48.5 131.6 %all-gather.11.cloned.1.call-start = ((), (), s32[]{:S(2)}) async-start(), calls=%async_computation.8 | async-start | bytes 2654208 | tf_op jit(solution)/shard_map/all_gather | solution.py:262
  49.1 269.5 %reduce-scatter.6.cloned.1.call-start = ((), (), s32[]{:S(2)}) async-start(), calls=%async_computation.9 | async-start | bytes 5013504 | tf_op jit(solution)/shard_map/reduce_scatter | solution.py:292
  132.7 4.4 copy-start
  141.3 47.8 %copy-start.6 = (f32[384,576]{0,1:T(8,128)}, f32[384,576]{0,1:T(8,128)S(1)}, u32[]{:S(2)}) copy-start(f32[384,576]{0,1:T(8,128)S(1)} %get-tuple-element.72) | copy-start | bytes 2654212
  180.1 6.3 %copy-start.10 = (bf16[576,3072]{1,0:T(8,128)(2,1)S(1)}, bf16[576,3072]{1,0:T(8,128)(2,1)}, u32[]{:S(2)}) copy-start(bf16[576,3072]{1,0:T(8,128)(2,1)} %all-gather.9.cloned.1.call-done) | copy-start | bytes 10616836
  186.4 2.7 copy-start.42
  186.4 2.8 copy-start.19
  186.4 2.8 copy-start.38
  199.7 3.4 copy-start.1
  241.5 2.8 copy-start.20
  241.5 95.9 %reduce-scatter.10.cloned.1.call-start = ((), (), s32[]{:S(2)}) async-start(), calls=%async_computation.11 | async-start | bytes 1105920 | tf_op jit(solution)/shard_map/reduce_scatter | solution.py:331
  244.3 124.3 %reduce-scatter.14.cloned.1.call-start = ((), (), s32[]{:S(2)}) async-start(), calls=%async_computation.13 | async-start | bytes 2654208 | tf_op jit(solution)/shard_map/reduce_scatter | solution.py:331
  247.9 170.6 %reduce-scatter.12.cloned.1.call-start = ((), (), s32[]{:S(2)}) async-start(), calls=%async_computation.12 | async-start | bytes 5308416 | tf_op jit(solution)/shard_map/reduce_scatter | solution.py:331
  254.7 188.5 %reduce-scatter.8.cloned.1.call-start = ((), (), s32[]{:S(2)}) async-start(), calls=%async_computation.10 | async-start | bytes 1769472 | tf_op jit(solution)/shard_map/reduce_scatter | solution.py:340
  258.6 5.5 copy-start.39
  261.7 3.1 copy-start.24
  261.7 3.1 copy-start.28
  265.0 55.6 %copy-start.18 = (f32[32,384]{0,1:T(8,128)S(1)}, f32[32,384]{0,1:T(8,128)}, u32[]{:S(2)}) copy-start(f32[32,384]{0,1:T(8,128)} %copy-done.17) | copy-start | bytes 147460
  265.0 55.6 %copy-start.25 = (f32[32,384]{0,1:T(8,128)S(1)}, f32[32,384]{0,1:T(8,128)}, u32[]{:S(2)}) copy-start(f32[32,384]{0,1:T(8,128)} %copy.117) | copy-start | bytes 147460
  326.3 228.1 %all-reduce.5.cloned.1.call-start = ((), (), s32[]{:S(2)}) async-start(), calls=%async_computation.14 | async-start | bytes 7225344 | tf_op jit(solution)/shard_map/psum | solution.py:341
  555.7 3.6 copy-start.8
  (21 other events, 31.3 us)
Sparse Core Ops, SparseCore 0:
  11.1 25.4 all-gather.4
  45.9 53.2 all-gather.6
  101.3 47.9 all-gather.8
  150.7 29.4 all-gather.10
  241.6 76.8 reduce-scatter.5
  321.4 15.9 reduce-scatter.9
  340.3 28.2 reduce-scatter.13
  370.8 47.6 reduce-scatter.11
  421.5 21.7 reduce-scatter.7
  447.2 107.2 all-reduce.4
